TPU v7x, 32 devices: a whole 2x2x4 slice. The times are simulated.
32 devices in a mesh: groups: 2 (over x), row: 8 (over z, y), col: 2 (over core).
Axes of the slice: x: 2, y: 2, z: 4, core: 2. Of those that a mesh axis runs over, the one named last changes fastest.
Arguments:
- vectors: bfloat16 [131072, 32], P(('groups', 'row')), parts along dimension 0, may hold values from -6 to 6
- coords: bfloat16 [3, 65536], P(None, 'row'), may hold values from 0 to 1
- sigma: bfloat16 [131072], P(('groups', 'row')), parts along dimension 0, may hold values from 0.079589844 to 0.796875
- counts: int32 [256], replicated, may hold values from 1 to 24, as said below
- columns: int32 [256, 24], replicated, may hold values from 0 to 255, as said below
Outputs:
- product_field: float32 [131072, 32], P(('groups', 'row', 'col')), parts along dimension 0
There are 2 independent parts, one for each index of `groups`. A program takes and returns all parts, laid end to end along the dimension named above; an argument that names none is the same for every part. Nothing has to cross between parts.
Inputs may be any that keep to these rules, and one draw needn't show every extreme that they name: counts[i] is at most min(24, 256 - i); block row 0 has exactly 24. `columns`: in block row i the first counts[i] entries are distinct, the first is i and the others lie between i + 1 and min(i + 96, 256) - 1; the entries past them equal i.
All inputs are finite; a program needn't handle non-finite values.
Results may differ from a plain program's by a relative error of at most 0.0029.
Values may be sent and summed in bfloat16 or wider, within the bound.
No kernel may reach another device: no remote copies, remote signals or barrier semaphores. Data moves between devices by JAX's collectives and lax.ppermute only.
A program may use at most 64 MiB of HBM per device.

v0:
```python
import math

import jax
import jax.numpy as jnp
from jax import lax
from jax.sharding import PartitionSpec as P

BLK = 256
NV = 32
KMAX = 24


corr_length = 0.12
support_radius = 0.3
nugget_share = 1.0
sqrt_three = math.sqrt(3.0)
tile_group = 8
reach_devices = 3


def from_behind(block, axis, distance):
    devices = range(lax.axis_size(axis))
    route = [(i - distance, i) for i in devices if i - distance in devices]
    return lax.ppermute(block, axis, route)


def kernel_block(points_row, spread_row, points_col, spread_col, diagonal_flag):
    size_row = points_row.shape[2]
    size_col = points_col.shape[2]
    squared = jnp.zeros((points_row.shape[0], size_row, size_col), jnp.float32)
    for component in range(3):
        offset = points_row[:, component, :, None] - points_col[:, component, None, :]
        squared = squared + offset * offset
    distance = jnp.sqrt(squared)
    scaled = sqrt_three * distance / corr_length
    matern = (1.0 + scaled) * jnp.exp(-scaled)
    ratio = distance / support_radius
    taper = jnp.maximum(1.0 - ratio, 0.0) ** 4 * (1.0 + 4.0 * ratio)
    values = spread_row[:, :, None] * spread_col[:, None, :] * matern * taper
    identity = (
        lax.broadcasted_iota(jnp.int32, (size_row, size_col), 0)
        == lax.broadcasted_iota(jnp.int32, (size_row, size_col), 1)
    ).astype(jnp.float32)
    weight = jnp.where(diagonal_flag, nugget_share, 0.0)
    extra = weight[:, None, None] * identity[None] * (spread_row * spread_row)[:, :, None]
    return (values + extra).astype(jnp.bfloat16)


def compact(row_local, col_local, active):
    flat_rows = row_local.reshape(-1)
    flat_cols = col_local.reshape(-1)
    flat_active = active.reshape(-1).astype(jnp.int32)
    total_slots = flat_rows.shape[0]
    position = jnp.where(flat_active > 0, jnp.cumsum(flat_active) - 1, total_slots)
    packed_rows = jnp.zeros((total_slots + 1,), jnp.int32).at[position].set(flat_rows)[:total_slots]
    packed_cols = jnp.zeros((total_slots + 1,), jnp.int32).at[position].set(flat_cols)[:total_slots]
    return (packed_rows, packed_cols, jnp.sum(flat_active))


def sweep(
    packed_rows, packed_cols, live_count, points, spreads, blocks, totals, mirror_from, mirror_upto
):
    total_slots = packed_rows.shape[0]

    def one_turn(turn_index, running):
        slot_ids = turn_index * tile_group + jnp.arange(tile_group, dtype=jnp.int32)
        usable = slot_ids < live_count
        slot_ids = jnp.minimum(slot_ids, total_slots - 1)
        row_ids = packed_rows[slot_ids]
        col_ids = packed_cols[slot_ids]
        tile_block = kernel_block(
            points[row_ids], spreads[row_ids], points[col_ids], spreads[col_ids], row_ids == col_ids
        )
        tile_block = jnp.where(usable[:, None, None], tile_block, jnp.zeros_like(tile_block))
        toward_rows = jnp.einsum(
            "gab,gbv->gav", tile_block, blocks[col_ids], preferred_element_type=jnp.float32
        )
        running = running.at[row_ids].add(toward_rows)
        mirrored = (row_ids != col_ids) & (col_ids >= mirror_from) & (col_ids < mirror_upto)
        toward_cols = jnp.einsum(
            "gab,gav->gbv", tile_block, blocks[row_ids], preferred_element_type=jnp.float32
        )
        running = running.at[col_ids].add(jnp.where(mirrored[:, None, None], toward_cols, 0.0))
        return running

    turns = (live_count + tile_group - 1) // tile_group
    return lax.fori_loop(0, turns, one_turn, totals)


def stacked(pieces, rows_dev):
    blocks = jnp.concatenate([item[0].reshape(rows_dev, BLK, NV) for item in pieces], axis=0)
    points = jnp.concatenate(
        [
            item[1].astype(jnp.float32).reshape(3, rows_dev, BLK).transpose(1, 0, 2)
            for item in pieces
        ],
        axis=0,
    )
    spreads = jnp.concatenate(
        [item[2].astype(jnp.float32).reshape(rows_dev, BLK) for item in pieces], axis=0
    )
    return (blocks, points, spreads)


def local(vectors, coords, sigma, counts, columns):
    cells_dev = vectors.shape[0]
    rows_dev = cells_dev // BLK
    first_row = lax.axis_index("row") * rows_dev
    core_index = lax.axis_index("col")
    half_slots = KMAX // 2
    own_columns = lax.dynamic_slice_in_dim(columns, first_row, rows_dev, 0)
    own_counts = lax.dynamic_slice_in_dim(counts, first_row, rows_dev, 0)
    picked = core_index * half_slots + jnp.arange(half_slots, dtype=jnp.int32)
    ahead = [(vectors, coords, sigma)]
    for stride in range(1, reach_devices + 1):
        ahead.append(from_behind((vectors, coords, sigma), "row", -stride))
    blocks, points, spreads = stacked(ahead, rows_dev)
    extent = (reach_devices + 1) * rows_dev
    row_local = jnp.broadcast_to(
        jnp.arange(rows_dev, dtype=jnp.int32)[:, None], (rows_dev, half_slots)
    )
    chosen_cols = jnp.take(own_columns, picked, axis=1) - first_row
    active = picked[None, :] < own_counts[:, None]
    packed_rows, packed_cols, live_count = compact(row_local, chosen_cols, active)
    empty = jnp.zeros((extent, BLK, NV), jnp.float32)
    totals = sweep(packed_rows, packed_cols, live_count, points, spreads, blocks, empty, 0, extent)
    own_part = totals[:rows_dev]
    for stride in range(1, reach_devices + 1):
        own_part = own_part + from_behind(
            totals[stride * rows_dev : (stride + 1) * rows_dev], "row", stride
        )
    return lax.psum_scatter(own_part.reshape(cells_dev, NV), "col", scatter_dimension=0, tiled=True)


def solution(mesh):
    in_specs = (P(("groups", "row"), None), P(None, "row"), P(("groups", "row")), P(), P())
    out_specs = P(("groups", "row", "col"), None)
    return jax.shard_map(local, mesh=mesh, in_specs=in_specs, out_specs=out_specs, check_vma=False)
```

profile of v0, /device:TPU:0, one launch (start us, length us, event | category | flops | bytes accessed | tf_op | source)
XLA Modules:
  0.0 1173.2 jit_solution(7285035238874716468)
XLA Ops:
  27.7 15.7 %collective-permute-done.1 = bf16[8192]{0:T(1024)(128)(2,1)S(1)} collective-permute-done((bf16[8192]{0:T(1024)(128)(2,1)}, bf16[8192]{0:T(1024)(128)(2,1)S(1)}, u32[]{:S(2)}, u32[]{:S(2)}) %collective-permute-start.1) | collective-permute-done | bytes 16416 | tf_op jit(solution)/shard_map/ppermute | solution.py:24
  46.0 4.6 collective-permute-done.5
  50.6 21.9 %collective-permute-done.4 = bf16[3,8192]{1,0:T(4,128)(2,1)S(1)} collective-permute-done((bf16[3,8192]{1,0:T(4,128)(2,1)}, bf16[3,8192]{1,0:T(4,128)(2,1)S(1)}, u32[]{:S(2)}, u32[]{:S(2)}) %collective-permute-start.4) | collective-permute-done | bytes 49184 | tf_op jit(solution)/shard_map/ppermute | solution.py:24
  74.0 6.1 copy.33
  82.6 1019.8 %while.12 = (s32[]{:T(128)}, f32[128,256,32]{1,2,0:T(8,128)}, s32[]{:T(128)}, s32[384]{0:T(512)S(1)}, s32[]{:T(128)}, /*index=5*/f32[128,256]{1,0:T(8,128)S(1)},...) while((s32[]{:T(128)}, f32[128,256,32]{1,2,0:T(8,128)}, ...), condition=%wide.region_8.9_spmd, body=%wide.region_5.8_spmd.sunk | while | flops 96801952 | bytes 4183117 | solution.py:87
  93.8 4.0 gather_fusion.7
  116.6 4.0 gather_fusion.7
  132.4 4.0 gather_fusion.2
  155.1 4.0 gather_fusion.2
  177.9 4.0 gather_fusion.2
  184.7 4.0 gather_fusion.7
  207.3 4.0 gather_fusion.7
  223.2 4.0 gather_fusion.2
  230.0 4.0 gather_fusion.7
  245.8 4.0 gather_fusion.2
  275.2 4.0 gather_fusion.7
  291.1 4.0 gather_fusion.2
  297.9 4.0 gather_fusion.7
  320.6 4.0 gather_fusion.7
  1106.0 6.2 collective-permute-start.11
  1114.1 4.1 collective-permute-done.9
  1118.2 6.3 collective-permute-done.11
  1124.5 11.2 collective-permute-done.10
  1138.5 27.9 %reduce-scatter.2.cloned.1.call-done = f32[4096,32]{0,1:T(8,128)} async-done(((f32[8192,32]{0,1:T(8,128)}), f32[4096,32]{0,1:T(8,128)}) %reduce-scatter.2.cloned.1.call-update) | async-done | bytes 524304 | tf_op jit(solution)/shard_map/reduce_scatter | solution.py:132
  (1261 shorter events, 992.7 us)
Async XLA Ops:
  6.5 7.4 copy-start
  6.5 1159.8 %reduce-scatter.2.cloned.1.call-start = ((), (), s32[]{:S(2)}) async-start(), calls=%async_computation.1 | async-start | bytes 1572864 | tf_op jit(solution)/shard_map/reduce_scatter | solution.py:132
  6.5 9.8 collective-permute-start
  8.0 9.7 collective-permute-start.2
  9.3 64.3 %collective-permute-start.6 = (bf16[8192,32]{0,1:T(8,128)(2,1)}, bf16[8192,32]{0,1:T(8,128)(2,1)S(1)}, u32[]{:S(2)}, u32[]{:S(2)}) collective-permute-start(bf16[8192,32]{0,1:T(8,128)(2,1)} %param.7), channel_id=1, source_target_pairs={{2,0},{4,2},{6,4},{8,6},{10,8},{12,10},{14,12},{3,1},{5,3},{7,5},{... | collective-permute-start | bytes 1572872 | tf_op jit(solution)/shard_map/ppermute | solution.py:24
  10.6 63.0 %collective-permute-start.8 = (bf16[8192,32]{0,1:T(8,128)(2,1)}, bf16[8192,32]{0,1:T(8,128)(2,1)S(1)}, u32[]{:S(2)}, u32[]{:S(2)}) collective-permute-start(bf16[8192,32]{0,1:T(8,128)(2,1)} %param.7), channel_id=1, source_target_pairs={{6,0},{8,2},{10,4},{12,6},{14,8},{7,1},{9,3},{11,5},{13,7},{15,9},... | collective-permute-start | bytes 1572872 | tf_op jit(solution)/shard_map/ppermute | solution.py:24
  11.9 61.8 %collective-permute-start.7 = (bf16[8192,32]{0,1:T(8,128)(2,1)}, bf16[8192,32]{0,1:T(8,128)(2,1)S(1)}, u32[]{:S(2)}, u32[]{:S(2)}) collective-permute-start(bf16[8192,32]{0,1:T(8,128)(2,1)} %param.7), channel_id=1, source_target_pairs={{4,0},{6,2},{8,4},{10,6},{12,8},{14,10},{5,1},{7,3},{9,5},{11,7},{... | collective-permute-start | bytes 1572872 | tf_op jit(solution)/shard_map/ppermute | solution.py:24
  16.4 27.0 %collective-permute-start.1 = (bf16[8192]{0:T(1024)(128)(2,1)}, bf16[8192]{0:T(1024)(128)(2,1)S(1)}, u32[]{:S(2)}, u32[]{:S(2)}) collective-permute-start(bf16[8192]{0:T(1024)(128)(2,1)} %param.9), channel_id=1, source_target_pairs={{4,0},{6,2},{8,4},{10,6},{12,8},{14,10},{5,1},{7,3},{9,5},{11,7},{... | collective-permute-start | bytes 49160 | tf_op jit(solution)/shard_map/ppermute | solution.py:24
  17.7 27.0 %collective-permute-start.3 = (bf16[3,8192]{1,0:T(4,128)(2,1)}, bf16[3,8192]{1,0:T(4,128)(2,1)S(1)}, u32[]{:S(2)}, u32[]{:S(2)}) collective-permute-start(bf16[3,8192]{1,0:T(4,128)(2,1)} %param.8), channel_id=1, source_target_pairs={{2,0},{4,2},{6,4},{8,6},{10,8},{12,10},{14,12},{3,1},{5,3},{7,5},{... | collective-permute-start | bytes 147464 | tf_op jit(solution)/shard_map/ppermute | solution.py:24
  43.4 7.3 collective-permute-start.5
  44.7 27.8 %collective-permute-start.4 = (bf16[3,8192]{1,0:T(4,128)(2,1)}, bf16[3,8192]{1,0:T(4,128)(2,1)S(1)}, u32[]{:S(2)}, u32[]{:S(2)}) collective-permute-start(bf16[3,8192]{1,0:T(4,128)(2,1)} %param.8), channel_id=1, source_target_pairs={{4,0},{6,2},{8,4},{10,6},{12,8},{14,10},{5,1},{7,3},{9,5},{11,7},{... | collective-permute-start | bytes 147464 | tf_op jit(solution)/shard_map/ppermute | solution.py:24
  1104.6 13.6 %collective-permute-start.9 = (f32[32,256,32]{1,2,0:T(8,128)S(1)}, f32[32,256,32]{1,2,0:T(8,128)S(1)}, u32[]{:S(2)}, u32[]{:S(2)}) collective-permute-start(f32[32,256,32]{1,2,0:T(8,128)S(1)} %get-tuple-element.173), channel_id=1, source_target_pairs={{0,2},{2,4},{4,6},{6,8},{8,10},{10,12},{12,14},{1,3},{3,5},{5,7},{... | collective-permute-start | bytes 3145736 | tf_op jit(solution)/shard_map/ppermute | solution.py:24
  1106.0 18.5 %collective-permute-start.11 = (f32[32,256,32]{1,2,0:T(8,128)S(1)}, f32[32,256,32]{1,2,0:T(8,128)S(1)}, u32[]{:S(2)}, u32[]{:S(2)}) collective-permute-start(f32[32,256,32]{1,2,0:T(8,128)S(1)} %get-tuple-element.174), channel_id=1, source_target_pairs={{0,6},{2,8},{4,10},{6,12},{8,14},{1,7},{3,9},{5,11},{7,13},{9,15},... | collective-permute-start | bytes 3145736 | tf_op jit(solution)/shard_map/ppermute | solution.py:24
  1112.2 23.5 %collective-permute-start.10 = (f32[32,256,32]{1,2,0:T(8,128)S(1)}, f32[32,256,32]{1,2,0:T(8,128)S(1)}, u32[]{:S(2)}, u32[]{:S(2)}) collective-permute-start(f32[32,256,32]{1,2,0:T(8,128)S(1)} %get-tuple-element.175), channel_id=1, source_target_pairs={{0,4},{2,6},{4,8},{6,10},{8,12},{10,14},{1,5},{3,7},{5,9},{7,11},{... | collective-permute-start | bytes 3145736 | tf_op jit(solution)/shard_map/ppermute | solution.py:24
Sparse Core Ops, SparseCore 0:
  1138.6 27.7 reduce-scatter.1
where the time goes:
time: 1190 us; the launch traced here: 1170 us
  local copies, waits for them, and re-layouts  548 us (46%)
  matrix products  250 us (21%)
  other arithmetic  243 us (20%)
  waiting for transfers between devices  91.7 us (8%)
  starting transfers between devices  21.2 us (2%)
  between operations  14.4 us (1%)
    gather x45, local copies, waits for them, and re-layouts, one_turn(): blocks[row_ids]  181 us
    gather x45, local copies, waits for them, and re-layouts, one_turn(): blocks[col_ids]  181 us
    dot_general x45, matrix products, one_turn(): jnp.einsum('gab,gav->gbv', tile_block, blocks[row_ids], preferred_element...  126 us
    dot_general x45, matrix products, one_turn(): jnp.einsum('gab,gbv->gav', tile_block, blocks[col_ids], preferred_element...  124 us
    scatter-add x45, other arithmetic, one_turn(): running = running.at[row_ids].add(toward_rows)  107 us
    scatter-add x45, other arithmetic, one_turn(): running.at[col_ids]  101 us
    ppermute x12, waiting for transfers between devices, from_behind(): return lax.ppermute(block, axis, route)  63.8 us
    gather x45, local copies, waits for them, and re-layouts, one_turn(): row_ids = packed_rows[slot_ids]  29.3 us
  transfers between devices with their start and end apart: 13, of which 7 were waited for; matrix products, arithmetic and copies ran while one was open for 1% of the time, Pallas kernels for 0%

commit v1 on v0

v1 whole, which is shorter than its diff:
```python
import functools
import math

import jax
import jax.numpy as jnp
from jax import lax
from jax.experimental import pallas as pl
from jax.experimental.pallas import tpu as pltpu
from jax.sharding import PartitionSpec as P

BLK = 256
NV = 32
KMAX = 24
FEAT = 16
REACH = 3
PIECES = 8
FILL = 64
CHUNK = 32

CORR = 0.12
SUPPORT = 0.3
SCALE = math.sqrt(3.0) / CORR * math.log2(math.e)
EDGE = SUPPORT * SCALE
SHIFT_U = 1.0 / math.log(2.0)
SHIFT_T = EDGE / 4.0
FACTOR = math.log(2.0) * 4.0 / EDGE**5 * 2.0**-EDGE


def split3(x):
    high = x.astype(jnp.bfloat16).astype(jnp.float32)
    rest = x - high
    mid = rest.astype(jnp.bfloat16).astype(jnp.float32)
    low = (rest - mid).astype(jnp.bfloat16).astype(jnp.float32)
    return [high, mid, low]


def message_kernel(vectors, coords_any, sigma_any, part, coords, sigma, rows, sems):
    half = vectors.shape[1] // 2
    core = lax.axis_index("col")
    begin = pl.multiple_of(core * half, half)
    copies = [
        pltpu.make_async_copy(coords_any, coords, sems.at[0]),
        pltpu.make_async_copy(sigma_any, sigma, sems.at[1]),
        pltpu.make_async_copy(vectors.at[:, pl.ds(begin, half)], part.at[:, pl.ds(0, half)], sems.at[2]),
    ]
    for copy in copies:
        copy.start()
    copies[0].wait()
    width = half // PIECES
    mine = coords[:, pl.ds(begin, half)].astype(jnp.float32)
    for axis in range(3):
        for piece in range(PIECES):
            rows[axis * PIECES + piece : axis * PIECES + piece + 1, :] = mine[
                axis : axis + 1, piece * width : (piece + 1) * width
            ]
    copies[1].wait()
    count = half // 128
    spread = sigma[pl.ds(pl.multiple_of(core * count, count), count), :].astype(jnp.float32)
    for row in range(count):
        piece, place = divmod(row * 128, width)
        rows[3 * PIECES + piece : 3 * PIECES + piece + 1, place : place + 128] = spread[row : row + 1, :]
    part[:, half:] = rows[...].astype(jnp.bfloat16)
    copies[2].wait()


def column_factors(points, spread, b_rows):
    norms = split3(SCALE * SCALE * (points[0:1] * points[0:1] + points[1:2] * points[1:2] + points[2:3] * points[2:3]))
    for index in range(3):
        b_rows[3 * index : 3 * index + 3, :] = points
        b_rows[9 + index : 10 + index, :] = norms[index]
    b_rows[12:15, :] = jnp.ones_like(points)
    if spread is not None:
        b_rows[15:16, :] = spread
    return norms


def unpack(message, rows, b_rows, b, w):
    half = b.shape[1]
    width = half // PIECES
    packed = message[:, half:].astype(jnp.float32)
    for row in range(4 * PIECES):
        index, piece = divmod(row, PIECES)
        rows[index : index + 1, piece * width : (piece + 1) * width] = packed[row : row + 1, :]
    column_factors(rows[0:3, :], rows[3:4, :], b_rows)
    b[...] = b_rows[...].astype(jnp.bfloat16)
    scaled(message[:, :half], rows[3:4, :], w)


def scaled(vectors, spread, out):
    product = vectors.astype(jnp.float32) * spread
    high = product.astype(jnp.bfloat16)
    out[0:NV, :] = high
    out[NV:, :] = (product - high.astype(jnp.float32)).astype(jnp.bfloat16)


def prepare_kernel(rows_dev, counts, columns, coords, sigma, vectors, out, a_out, b_out, w_out, b_rows, a_rows):
    points = coords[...].astype(jnp.float32)
    norms = column_factors(points, None, b_rows)
    cross = split3(-2.0 * SCALE * SCALE * points)
    a_rows[...] = jnp.zeros_like(a_rows)
    a_rows[9:12, :] = jnp.ones_like(points)
    for index in range(3):
        a_rows[3 * index : 3 * index + 3, :] = cross[index]
        a_rows[12 + index : 13 + index, :] = norms[index]
    spread = sigma[...].astype(jnp.float32)
    for row in range(sigma.shape[0]):
        piece = spread[row : row + 1, :]
        b_rows[15:16, row * 128 : (row + 1) * 128] = piece
    b_out[...] = b_rows[...].astype(jnp.bfloat16)
    scaled(vectors[...], b_rows[15:16, :], w_out)
    for block in range(rows_dev):
        cells = slice(block * BLK, (block + 1) * BLK)
        a_out[cells, :] = a_rows[:, cells].T.astype(jnp.bfloat16)
    half = rows_dev // 2
    core = lax.axis_index("col")
    total = rows_dev * KMAX
    first_row = lax.axis_index("row") * rows_dev
    window = columns[:, pl.ds(pl.multiple_of((first_row >> 7) * 128, 128), 128)]
    window = pltpu.roll(window, (128 - (first_row & 127)) & 127, 1)
    window = jnp.concatenate([window, jnp.zeros((128 - KMAX, 128), jnp.int32)], axis=0)
    ahead = window.astype(jnp.float32).T[0:rows_dev].astype(jnp.int32) - first_row
    row = lax.broadcasted_iota(jnp.int32, ahead.shape, 0)
    slot = lax.broadcasted_iota(jnp.int32, ahead.shape, 1)
    live_slots = jnp.zeros(ahead.shape, jnp.int32)
    for index in range(rows_dev):
        live_slots = jnp.where(row == index, counts[first_row + index], live_slots)
    step = ahead >> 5
    col = ahead & 31
    live = (slot < live_slots) & (ahead != row)
    local = step == 0
    same_half = (row >> 4) == (col >> 4)
    mine = (col >> 4) == core
    phase = jnp.where(local, jnp.where(same_half, 4, 0), step)
    phase = jnp.where(mine | (phase == 0), phase, 5)
    phase = jnp.where(live, phase, 6)
    phase = jnp.where(slot < KMAX, phase, 99)
    code = row * 64 + jnp.where(local, col, col & (half - 1))
    stack = jnp.concatenate([(phase == index).astype(jnp.float32) for index in range(8)], axis=0).astype(jnp.bfloat16)
    size = stack.shape[0]
    width = ahead.shape[1]

    def order(shape, first, second):
        return (
            lax.broadcasted_iota(jnp.int32, shape, first) < lax.broadcasted_iota(jnp.int32, shape, second)
        ).astype(jnp.float32).astype(jnp.bfloat16)

    in_row = jnp.dot(stack, order((width, width), 0, 1), preferred_element_type=jnp.float32)
    row_sum = jnp.dot(stack, jnp.ones((width, width), jnp.bfloat16), preferred_element_type=jnp.float32)
    above = jnp.dot(order((size, size), 1, 0), row_sum.astype(jnp.bfloat16), preferred_element_type=jnp.float32)
    rank = jnp.full(ahead.shape, -1.0, jnp.float32)
    for index in range(8):
        rows = slice(index * rows_dev, (index + 1) * rows_dev)
        rank = jnp.where(phase == index, in_row[rows] + above[rows], rank)
    rank = rank.astype(jnp.int32)
    place = lax.broadcasted_iota(jnp.int32, (rows_dev, total), 1)
    codes = code.astype(jnp.float32)
    picked = jnp.zeros((rows_dev, total), jnp.float32)
    for index in range(KMAX):
        picked = picked + jnp.where(rank[:, index : index + 1] == place, codes[:, index : index + 1], 0.0)
    out[0:1, 0:total] = jnp.sum(picked, axis=0, keepdims=True).astype(jnp.int32)
    chosen = lax.broadcasted_iota(jnp.int32, above.shape, 0) == rows_dev * lax.broadcasted_iota(jnp.int32, above.shape, 1)
    out[0:1, total : total + width] = jnp.sum(jnp.where(chosen, above, 0.0), axis=0, keepdims=True).astype(jnp.int32)


def phase_run(meta, rows_dev, phase):
    base = rows_dev * KMAX
    first = meta[0, base + phase]
    size = meta[0, base + phase + 1] - first
    if phase == 0:
        mine = meta[0, base + 5] - meta[0, base + 1]
        other = meta[0, base + 6] - meta[0, base + 5]
        core = lax.axis_index("col")
        load0 = jnp.where(core == 0, mine, other)
        load1 = jnp.where(core == 0, other, mine)
        lead = jnp.clip((load1 - load0 + size) >> 1, 0, size)
        first = jnp.where(core == 0, 0, lead)
        size = jnp.where(core == 0, lead, size - lead)
    return first, size


def lanes(index):
    return pl.ds(pl.multiple_of(index * BLK, BLK), BLK)


def fill_tile(dist, tile, slot):
    for chunk in range(BLK // CHUNK):
        rows = pl.ds(chunk * CHUNK, CHUNK)
        square = jnp.maximum(dist[slot, rows], 1e-12)
        rho = square * lax.rsqrt(square)
        inner = jnp.maximum(EDGE - rho, 0.0)
        inner2 = inner * inner
        shape = (inner2 * inner2) * ((rho + SHIFT_U) * (rho + SHIFT_T)) * jnp.exp2(inner)
        tile[slot, rows] = shape.astype(jnp.bfloat16)


def sweep(size, entry, a_ref, row_ref, col_ref, b_ref, dist, tile, add_row, add_col):
    def distances(step, slot):
        i, j = entry(step)
        dist[slot] = jnp.dot(a_ref[lanes(i), :], b_ref[:, lanes(j)], preferred_element_type=jnp.float32)

    @pl.when(size > 0)
    def _():
        distances(0, 0)

    def two_steps(turn, carry):
        additions = []
        for slot in range(2):
            step = turn * 2 + slot
            i, j = entry(step - 1)
            live = (step >= 1) & (step <= size)
            block = tile[1 - slot]
            toward_row = lax.dot_general(
                col_ref[:, lanes(j)], block, (((1,), (1,)), ((), ())), preferred_element_type=jnp.float32
            )
            additions.append((add_row, i, live, toward_row))
            if add_col is not None:
                toward_col = jnp.dot(row_ref[:, lanes(i)], block, preferred_element_type=jnp.float32)
                additions.append((add_col, j, live, toward_col))
            fill_tile(dist, tile, slot)
            distances(step + 1, 1 - slot)
        for add, block, live, value in additions:
            add(block, live, value[:NV] + value[NV:])
        return carry

    lax.fori_loop(0, jnp.where(size > 0, (size + 2) // 2, 0), two_steps, 0)


def adder(acc, spare, index):
    def add(block, live, value):
        where = lanes(jnp.where(live, index(block), spare))
        acc[:, where] = acc[:, where] + value

    return add


def listed(meta, start, size):
    def entry(step):
        code = meta[0, start + jnp.clip(step, 0, jnp.maximum(size - 1, 0))]
        return code >> 6, code & 63

    return size, entry


def diagonal_blocks(rows_dev, core):
    half = rows_dev // 2

    def entry(step):
        block = core * half + jnp.clip(step, 0, half - 1)
        return block, block

    return entry


def near_kernel(rows_dev, meta, a_ref, w_ref, b_ref, acc, dist, tile):
    half = rows_dev // 2
    core = lax.axis_index("col")
    acc[...] = jnp.zeros_like(acc)
    add = adder(acc, rows_dev, lambda block: block ^ (core * half))
    sweep(half, diagonal_blocks(rows_dev, core), a_ref, w_ref, w_ref, b_ref, dist, tile, add, None)


def ahead_kernel(phase, rows_dev, meta, a_ref, w_ref, message, before, *refs):
    half = rows_dev // 2
    core = lax.axis_index("col")
    if phase == 1:
        kept, given, back, dist, tile, acc_col, rows, b_rows, b, w, acc = refs
    elif phase == 3:
        b_ref, back2, acc, back, dist, tile, acc_col, rows, b_rows, b, w = refs
    else:
        b_ref, acc, back, dist, tile, acc_col, rows, b_rows, b, w = refs
    acc[...] = before[...]
    acc_col[...] = jnp.zeros_like(acc_col)
    if phase == 2:
        unpack(message, rows, b_rows, b, w)
    else:
        unpack(message.at[pl.ds(0 if phase == 1 else NV, NV)], rows, b_rows, b, w)
    add_row = adder(acc, rows_dev, lambda block: block ^ (core * half))
    add_col = adder(acc_col, half, lambda block: block)
    size, entry = listed(meta, *phase_run(meta, rows_dev, phase))
    sweep(size, entry, a_ref, w_ref, w, b, dist, tile, add_row, add_col)
    if phase != 1:
        start, size = phase_run(meta, rows_dev, 0)
        early = jnp.clip(FILL - phase_run(meta, rows_dev, 2)[1], 0, size)
        if phase == 2:
            size = early
        else:
            start, size = start + early, size - early
        size, entry = listed(meta, start, size)
        sweep(size, entry, a_ref, w_ref, w_ref, b_ref, dist, tile, add_row, add_row)
    sums = acc_col[:, : half * BLK].astype(back.dtype)
    if phase == 3:
        back[0:NV, :] = back2[...]
        back[NV:, :] = sums
    else:
        back[...] = sums
    if phase == 1:
        kept[...] = acc[:, : half * BLK]
        given[...] = acc[:, half * BLK : 2 * half * BLK]


def join_kernel(own, got, out):
    out[0:NV, :] = own[...]
    out[NV:, :] = got[...]


def onward_kernel(back, got, out):
    out[...] = (back[...] + got[NV:, :].astype(jnp.float32)).astype(out.dtype)


def inside_kernel(rows_dev, meta, a_ref, w_ref, b_ref, kept, got, vectors, out, scale, dist, tile, acc):
    half = rows_dev // 2
    acc[:, : half * BLK] = kept[...] + got[0:NV, :].astype(jnp.float32)
    acc[:, half * BLK :] = jnp.zeros((NV, BLK), jnp.float32)
    add = adder(acc, half, lambda block: block & (half - 1))
    size, entry = listed(meta, *phase_run(meta, rows_dev, 4))
    sweep(size, entry, a_ref, w_ref, w_ref, b_ref, dist, tile, add, add)
    width = half * BLK
    mine = pl.ds(pl.multiple_of(lax.axis_index("col") * width, width), width)
    spread = b_ref[:, mine].astype(jnp.float32)[FEAT - 1 : FEAT, :]
    scale[...] = FACTOR * spread
    out[...] = acc[:, :width] * (FACTOR * spread) + spread * spread * vectors[:, mine].astype(jnp.float32)


def estimate(microseconds):
    return pl.CostEstimate(flops=int(microseconds * 1.15e9), bytes_accessed=1 << 20, transcendentals=0)


def run(kernel, name, tiles, out_shape, scratch, operands):
    smem = pl.BlockSpec(memory_space=pltpu.SMEM)
    vmem = pl.BlockSpec(memory_space=pltpu.VMEM)
    multiple = isinstance(out_shape, tuple)
    return pl.pallas_call(
        kernel,
        out_shape=out_shape,
        in_specs=[smem] + [vmem] * (len(operands) - 1),
        out_specs=tuple(vmem for _ in out_shape) if multiple else vmem,
        scratch_shapes=[
            pltpu.VMEM((2, BLK, BLK), jnp.float32),
            pltpu.VMEM((2, BLK, BLK), jnp.bfloat16),
        ]
        + scratch,
        compiler_params=pltpu.CompilerParams(vmem_limit_bytes=28 * 1024 * 1024),
        cost_estimate=estimate(0.17 * tiles),
        name=name,
    )(*operands)


def local(vectors, coords, sigma, counts, columns):
    cells = vectors.shape[0]
    rows_dev = cells // BLK
    half_cells = cells // 2
    row_devices = lax.axis_size("row")
    smem = pl.BlockSpec(memory_space=pltpu.SMEM)
    vmem = pl.BlockSpec(memory_space=pltpu.VMEM)
    own = vectors.T
    sigma = sigma.reshape(cells // 128, 128)

    part = pl.pallas_call(
        message_kernel,
        out_shape=jax.ShapeDtypeStruct((NV, half_cells + half_cells // PIECES), jnp.bfloat16),
        in_specs=[pl.BlockSpec(memory_space=pltpu.HBM)] * 3,
        out_specs=vmem,
        scratch_shapes=[
            pltpu.VMEM(coords.shape, jnp.bfloat16),
            pltpu.VMEM(sigma.shape, jnp.bfloat16),
            pltpu.VMEM((4 * PIECES, half_cells // PIECES), jnp.float32),
            pltpu.SemaphoreType.DMA((3,)),
        ],
        compiler_params=pltpu.CompilerParams(vmem_limit_bytes=60 * 1024 * 1024),
        cost_estimate=estimate(2.0),
        name="message",
    )(own, coords, sigma)

    def from_ahead(block, stride):
        return lax.ppermute(block, "row", [(i + stride, i) for i in range(row_devices - stride)])

    def to_ahead(block, stride):
        return lax.ppermute(block, "row", [(i, i + stride) for i in range(row_devices - stride)])

    ahead2 = from_ahead(part, 2)
    joined = pl.pallas_call(
        join_kernel,
        out_shape=jax.ShapeDtypeStruct((2 * NV, part.shape[1]), part.dtype),
        in_specs=[vmem, vmem],
        out_specs=vmem,
        compiler_params=pltpu.CompilerParams(vmem_limit_bytes=28 * 1024 * 1024),
        cost_estimate=estimate(0.5),
        name="joined",
    )(part, ahead2)
    ahead13 = from_ahead(joined, 1)

    meta, a, b, w = pl.pallas_call(
        functools.partial(prepare_kernel, rows_dev),
        out_shape=(
            jax.ShapeDtypeStruct((1, rows_dev * KMAX + 128), jnp.int32),
            jax.ShapeDtypeStruct((cells, FEAT), jnp.bfloat16),
            jax.ShapeDtypeStruct((FEAT, cells), jnp.bfloat16),
            jax.ShapeDtypeStruct((2 * NV, cells), jnp.bfloat16),
        ),
        in_specs=[smem] + [vmem] * 4,
        out_specs=(vmem,) * 4,
        scratch_shapes=[pltpu.VMEM((FEAT, cells), jnp.float32)] * 2,
        compiler_params=pltpu.CompilerParams(vmem_limit_bytes=28 * 1024 * 1024),
        cost_estimate=estimate(4.0),
        name="prepare",
    )(counts, columns.T, coords, sigma, own)

    acc_shape = jax.ShapeDtypeStruct((NV, cells + BLK), jnp.float32)
    half_shape = jax.ShapeDtypeStruct((NV, half_cells), jnp.float32)
    back_shape = jax.ShapeDtypeStruct((NV, half_cells), jnp.bfloat16)
    spare = [
        pltpu.VMEM((NV, half_cells + BLK), jnp.float32),
        pltpu.VMEM((8, half_cells), jnp.float32),
        pltpu.VMEM((FEAT, half_cells), jnp.float32),
        pltpu.VMEM((FEAT, half_cells), jnp.bfloat16),
        pltpu.VMEM((2 * NV, half_cells), jnp.bfloat16),
    ]

    def ahead(phase, tiles, out_shape, scratch, *operands):
        kernel = functools.partial(ahead_kernel, phase, rows_dev)
        return run(kernel, "ahead%d" % phase, tiles, out_shape, spare + scratch, (meta, a, w) + operands)

    acc = run(functools.partial(near_kernel, rows_dev), "near", 16, acc_shape, [], (meta, a, w, b))
    acc, back2 = ahead(2, 75, (acc_shape, back_shape), [], ahead2, acc, b)
    backs_shape = jax.ShapeDtypeStruct((2 * NV, half_cells), jnp.bfloat16)
    acc, backs = ahead(3, 60, (acc_shape, backs_shape), [], ahead13, acc, b, back2)
    got = to_ahead(backs, 2)
    acc_row = [pltpu.VMEM((NV, cells + BLK), jnp.float32)]
    kept, given, back1 = ahead(1, 75, (half_shape, half_shape, half_shape), acc_row, ahead13, acc)
    onward = pl.pallas_call(
        onward_kernel,
        out_shape=back_shape,
        in_specs=[vmem, vmem],
        out_specs=vmem,
        compiler_params=pltpu.CompilerParams(vmem_limit_bytes=28 * 1024 * 1024),
        cost_estimate=estimate(0.5),
        name="onward",
    )(back1, got)
    given, onward = lax.optimization_barrier((given, onward))
    got1 = to_ahead(onward, 1)
    partner = lax.ppermute(given, "col", [(0, 1), (1, 0)])
    inner, scale = run(
        functools.partial(inside_kernel, rows_dev),
        "inside",
        18,
        (half_shape, jax.ShapeDtypeStruct((1, half_cells), jnp.float32)),
        [pltpu.VMEM((NV, half_cells + BLK), jnp.float32)],
        (meta, a, w, b, kept, got, own),
    )
    return (inner + (partner + got1.astype(jnp.float32)) * scale).T


def solution(mesh):
    in_specs = (P(("groups", "row"), None), P(None, "row"), P(("groups", "row")), P(), P())
    out_specs = P(("groups", "row", "col"), None)
    return jax.shard_map(local, mesh=mesh, in_specs=in_specs, out_specs=out_specs, check_vma=False)
```

time: 1190 us -> 76.9 us (0.06); the launches traced: 1170 us -> 76.6 us
  local copies, waits for them, and re-layouts: 548 us -> 0.02 us
  matrix products: 250 us -> 0 us
  other arithmetic: 243 us -> 0.89 us
  waiting for transfers between devices: 91.7 us -> 6.18 us
  Pallas kernels: 0 us -> 56.5 us
  between operations: 14.4 us -> 0.17 us
    gather x361 -> x0, local copies, waits for them, and re-layouts: 524 us -> none  [the longest x45 181 us: one_turn(): blocks[row_ids]]
    dot_general x90 -> x0, matrix products: 250 us -> none  [the longest x45 126 us: one_turn(): jnp.einsum('gab,gav->gbv', tile_block, blocks[row_ids], preferred_element...]
    scatter-add x90 -> x0, other arithmetic: 208 us -> none  [the longest x45 107 us: one_turn(): running = running.at[row_ids].add(toward_rows)]
    ppermute x12 -> x5, waiting for transfers between devices: 63.8 us -> 6.18 us  [the longest x2 4.78 us: from_ahead(): lax.ppermute(block, 'row', [(i + stride, i) for i in range(row_devices -...]
    pallas_call x0 -> x9, Pallas kernels: none -> 56.5 us  [the longest x5 52.1 us: run(): pl.pallas_call(kernel, out_shape=out_shape, in_specs=[smem] + [vmem] * (l...]
    reduce_scatter x1 -> x0, waiting for transfers between devices: 27.9 us -> none  [local(): lax.psum_scatter(own_part.reshape(cells_dev, NV), 'col', scatter_dimensio...]
    and x46 -> x0, other arithmetic: 27.5 us -> none  [the longest x45 27.4 us: one_turn(): (row_ids != col_ids) & (col_ids >= mirror_from) & (col_ids < mirror_upto)]
  transfers between devices with their start and end apart: 13 -> 5, of which waited for: 7 -> 2; matrix products, arithmetic and copies ran while one was open for 1% -> 0% of each run, Pallas kernels for 0% -> 58%
where the time goes in v1:
time: 76.9 us; the launch traced here: 76.6 us
  Pallas kernels  56.5 us (73%)
  starting transfers between devices  12.9 us (17%)
  waiting for transfers between devices  6.18 us (8%)
  other arithmetic  0.89 us (1%)
    pallas_call x5, Pallas kernels, run(): pl.pallas_call(kernel, out_shape=out_shape, in_specs=[smem] + [vmem] * (l...  52.1 us
    ppermute x2, starting transfers between devices, to_ahead(): lax.ppermute(block, 'row', [(i, i + stride) for i in range(row_devices -...  10.2 us
    ppermute x2, waiting for transfers between devices, from_ahead(): lax.ppermute(block, 'row', [(i + stride, i) for i in range(row_devices -...  4.78 us
    ppermute x2, starting transfers between devices, from_ahead(): lax.ppermute(block, 'row', [(i + stride, i) for i in range(row_devices -...  2.58 us
    pallas_call x1, Pallas kernels, local(): pl.pallas_call(functools.partial(prepare_kernel, rows_dev), out_shape=(ja...  2.51 us
    pallas_call x1, Pallas kernels, local(): pl.pallas_call(message_kernel, out_shape=jax.ShapeDtypeStruct((NV, half_c...  1.8 us
  transfers between devices with their start and end apart: 5, of which 2 were waited for; matrix products, arithmetic and copies ran while one was open for 0% of the time, Pallas kernels for 58%

profile of v1, /device:TPU:0, one launch (start us, length us, event | category | flops | bytes accessed | tf_op | source)
XLA Modules:
  0.0 76.6 jit_solution(14956151655457410000)
XLA Ops:
  0.0 1.8 %message.1.own = bf16[32,4608]{1,0:T(8,128)(2,1)} custom-call(bf16[32,8192]{1,0:T(8,128)(2,1)} %bitcast.7, bf16[3,8192]{1,0:T(4,128)(2,1)} %coords_any.1, bf16[64,128]{1,0:T(8,128)(2,1)} %bitcast.11), custom_call_target="tpu_custom_call" | custom-call | flops 2300000000 | bytes 1048576 | tf_op jit(solution)/shard_map/message/pallas_call | solution.py:358
  1.8 1.3 %collective-permute-start = (bf16[32,4608]{1,0:T(8,128)(2,1)}, bf16[32,4608]{1,0:T(8,128)(2,1)S(1)}, u32[]{:S(2)}, u32[]{:S(2)}) collective-permute-start(bf16[32,4608]{1,0:T(8,128)(2,1)} %message.1.own), channel_id=1, source_target_pairs={{4,0},{6,2},{8,4},{10,6},{12,8},{14,10},{5,1},{7,3},{9,5},{11,7},{... | collective-permute-start | bytes 884744 | tf_op jit(solution)/shard_map/ppermute | solution.py:375
  3.1 0.0 copy-done
  3.1 0.0 copy-done.2
  3.1 0.0 copy-done.3
  3.2 0.0 copy-done.4
  3.2 0.0 copy-done.5
  3.2 2.5 %prepare.1 = (s32[1,896]{1,0:T(1,128)S(1)}, bf16[8192,16]{1,0:T(8,128)(2,1)S(1)}, bf16[16,8192]{1,0:T(8,128)(2,1)S(1)}, bf16[64,8192]{1,0:T(8,128)(2,1)S(1)}) custom-call(s32[256]{0:T(256)S(1)} %copy-done.5, s32[24,256]{1,0:T(8,128)S(1)} %bitcast.10, bf16[3,8192]{1,0:T(4,128)(2,1)S(1)} %copy-done.2, bf16[64,128]{1,0:T(8,128)(2,1)S(1)} %bitcast.12, ...), custom_call_target="tpu_custom_call" | custom-call | flops 4600000000 | bytes 1048576 | tf_op jit(solution)/shard_map/prepare/pallas_call | solution.py:392
  5.7 0.0 copy-start.1
  5.7 3.5 %near.1.before = f32[32,8448]{1,0:T(8,128)S(1)} custom-call(s32[1,896]{1,0:T(1,128)S(1)} %get-tuple-element.20.meta, bf16[8192,16]{1,0:T(8,128)(2,1)S(1)} %get-tuple-element.21.a_ref, bf16[64,8192]{1,0:T(8,128)(2,1)S(1)} %get-tuple-element.22.w_ref, bf16[16,8192]{1,0:T(8,128)(2,1)S(1)} %get-tuple-element.23.b_ref.refs_0_), custom_call_target="tpu_custom_call" | custom-call | flops 3128000000 | bytes 1048576 | tf_op jit(solution)/shard_map/near/pallas_call | solution.py:332
  9.2 4.8 %collective-permute-done.got.message = bf16[32,4608]{1,0:T(8,128)(2,1)S(1)} collective-permute-done((bf16[32,4608]{1,0:T(8,128)(2,1)}, bf16[32,4608]{1,0:T(8,128)(2,1)S(1)}, u32[]{:S(2)}, u32[]{:S(2)}) %collective-permute-start) | collective-permute-done | bytes 294944 | tf_op jit(solution)/shard_map/ppermute | solution.py:375
  14.0 1.3 %collective-permute-start.1 = (bf16[64,4608]{1,0:T(8,128)(2,1)S(1)}, bf16[64,4608]{1,0:T(8,128)(2,1)S(1)}, u32[]{:S(2)}, u32[]{:S(2)}) collective-permute-start(bf16[64,4608]{1,0:T(8,128)(2,1)S(1)} %joined.1), channel_id=1, source_target_pairs={{2,0},{4,2},{6,4},{8,6},{10,8},{12,10},{14,12},{3,1},{5,3},{7,5},{... | collective-permute-start | bytes 1769480 | tf_op jit(solution)/shard_map/ppermute | solution.py:375
  15.3 16.8 %ahead2.1 = (f32[32,8448]{1,0:T(8,128)S(1)}, bf16[32,4096]{1,0:T(8,128)(2,1)S(1)}) custom-call(s32[1,896]{1,0:T(1,128)S(1)} %get-tuple-element.20.meta, bf16[8192,16]{1,0:T(8,128)(2,1)S(1)} %get-tuple-element.21.a_ref, bf16[64,8192]{1,0:T(8,128)(2,1)S(1)} %get-tuple-element.22.w_ref, bf16[32,4608]{1,0:T(8,128)(2,1)S(1)} %collective-permute-done.got.message, ...), custom_call_target="tpu_custom_call" | custom-call | flops 14662500352 | bytes 1048576 | tf_op jit(solution)/shard_map/ahead2/pallas_call | solution.py:332
  32.1 0.0 collective-permute-done.1.message
  32.1 9.9 %ahead3.1 = (f32[32,8448]{1,0:T(8,128)S(1)}, bf16[64,4096]{1,0:T(8,128)(2,1)S(1)}) custom-call(s32[1,896]{1,0:T(1,128)S(1)} %get-tuple-element.20.meta, bf16[8192,16]{1,0:T(8,128)(2,1)S(1)} %get-tuple-element.21.a_ref, bf16[64,8192]{1,0:T(8,128)(2,1)S(1)} %get-tuple-element.22.w_ref, bf16[64,4608]{1,0:T(8,128)(2,1)S(1)} %collective-permute-done.1.message, ...), custom_call_target="tpu_custom_call" | custom-call | flops 11729999872 | bytes 1048576 | tf_op jit(solution)/shard_map/ahead3/pallas_call | solution.py:332
  42.0 8.4 %collective-permute-start.2 = (bf16[64,4096]{1,0:T(8,128)(2,1)S(1)}, bf16[64,4096]{1,0:T(8,128)(2,1)S(1)}, u32[]{:S(2)}, u32[]{:S(2)}) collective-permute-start(bf16[64,4096]{1,0:T(8,128)(2,1)S(1)} %get-tuple-element.28), channel_id=1, source_target_pairs={{0,4},{2,6},{4,8},{6,10},{8,12},{10,14},{1,5},{3,7},{5,9},{7,11},{... | collective-permute-start | bytes 1572872 | tf_op jit(solution)/shard_map/ppermute | solution.py:378
  50.5 17.1 %ahead1.1 = (f32[32,4096]{1,0:T(8,128)S(1)}, f32[32,4096]{1,0:T(8,128)S(1)}, f32[32,4096]{1,0:T(8,128)S(1)}) custom-call(s32[1,896]{1,0:T(1,128)S(1)} %get-tuple-element.20.meta, bf16[8192,16]{1,0:T(8,128)(2,1)S(1)} %get-tuple-element.21.a_ref, bf16[64,8192]{1,0:T(8,128)(2,1)S(1)} %get-tuple-element.22.w_ref, ...), custom_call_target="tpu_custom_call" | custom-call | flops 14662500352 | bytes 1048576 | tf_op jit(solution)/shard_map/ahead1/pallas_call | solution.py:332
  67.6 0.0 collective-permute-done.2.got
  67.7 0.1 collective-permute-start.3
  67.8 1.8 %collective-permute-start.4 = (bf16[32,4096]{1,0:T(8,128)(2,1)S(1)}, bf16[32,4096]{1,0:T(8,128)(2,1)S(1)}, u32[]{:S(2)}, u32[]{:S(2)}) collective-permute-start(bf16[32,4096]{1,0:T(8,128)(2,1)S(1)} %onward.1), channel_id=1, source_target_pairs={{0,2},{2,4},{4,6},{6,8},{8,10},{10,12},{12,14},{1,3},{3,5},{5,7},{... | collective-permute-start | bytes 786440 | tf_op jit(solution)/shard_map/ppermute | solution.py:378
  69.6 4.8 %inside.1 = (f32[32,4096]{1,0:T(8,128)S(1)}, f32[1,4096]{1,0:T(1,128)S(1)}) custom-call(s32[1,896]{1,0:T(1,128)S(1)} %get-tuple-element.20.meta, bf16[8192,16]{1,0:T(8,128)(2,1)S(1)} %get-tuple-element.21.a_ref, bf16[64,8192]{1,0:T(8,128)(2,1)S(1)} %get-tuple-element.22.w_ref, bf16[16,8192]{1,0:T(8,128)(2,1)S(1)} %get-tuple-element.23.b_ref.refs_0_, ...), custom_call_target="tpu_custom_call" | custom-call | flops 3519000064 | bytes 1048576 | tf_op jit(solution)/shard_map/inside/pallas_call | solution.py:332
  74.3 1.4 %collective-permute-done.4 = bf16[32,4096]{1,0:T(8,128)(2,1)S(1)} collective-permute-done((bf16[32,4096]{1,0:T(8,128)(2,1)S(1)}, bf16[32,4096]{1,0:T(8,128)(2,1)S(1)}, u32[]{:S(2)}, u32[]{:S(2)}) %collective-permute-start.4) | collective-permute-done | bytes 262176 | tf_op jit(solution)/shard_map/ppermute | solution.py:378
  75.7 0.0 collective-permute-done.3
  75.7 0.9 %add_bitcast_fusion = f32[4096,32]{0,1:T(8,128)} fusion(f32[32,4096]{1,0:T(8,128)S(1)} %get-tuple-element.29, f32[32,4096]{1,0:T(8,128)S(1)} %collective-permute-done.3, bf16[32,4096]{1,0:T(8,128)(2,1)S(1)} %collective-permute-done.4, f32[4096]{0:T(1024)S(1)} %bitcast.6), kind=kLoop, calls=%fused_computation | loop fusion | flops 524288 | bytes 1851392 | tf_op jit(solution)/shard_map/transpose | solution.py:450
  (8 shorter events, 0.1 us)
Async XLA Ops:
  0.0 3.1 %copy-start = (bf16[8192,32]{0,1:T(8,128)(2,1)S(1)}, bf16[8192,32]{0,1:T(8,128)(2,1)}, u32[]{:S(2)}) copy-start(bf16[8192,32]{0,1:T(8,128)(2,1)} %param.5) | copy-start | bytes 1572868
  0.0 3.1 %copy-start.2 = (bf16[3,8192]{1,0:T(4,128)(2,1)S(1)}, bf16[3,8192]{1,0:T(4,128)(2,1)}, u32[]{:S(2)}) copy-start(bf16[3,8192]{1,0:T(4,128)(2,1)} %coords_any.1) | copy-start | bytes 147460
  0.0 3.1 %copy-start.3 = (s32[256,24]{0,1:T(8,128)S(1)}, s32[256,24]{0,1:T(8,128)}, u32[]{:S(2)}) copy-start(s32[256,24]{0,1:T(8,128)} %param.9) | copy-start | bytes 73732
  0.0 3.1 %copy-start.4 = (bf16[8192]{0:T(1024)(128)(2,1)S(1)}, bf16[8192]{0:T(1024)(128)(2,1)}, u32[]{:S(2)}) copy-start(bf16[8192]{0:T(1024)(128)(2,1)} %param.7) | copy-start | bytes 49156
  0.0 3.2 %copy-start.5 = (s32[256]{0:T(256)S(1)}, s32[256]{0:T(256)}, u32[]{:S(2)}) copy-start(s32[256]{0:T(256)} %counts.1) | copy-start | bytes 3076
  1.8 12.2 %collective-permute-start = (bf16[32,4608]{1,0:T(8,128)(2,1)}, bf16[32,4608]{1,0:T(8,128)(2,1)S(1)}, u32[]{:S(2)}, u32[]{:S(2)}) collective-permute-start(bf16[32,4608]{1,0:T(8,128)(2,1)} %message.1.own), channel_id=1, source_target_pairs={{4,0},{6,2},{8,4},{10,6},{12,8},{14,10},{5,1},{7,3},{9,5},{11,7},{... | collective-permute-start | bytes 884744 | tf_op jit(solution)/shard_map/ppermute | solution.py:375
  5.7 8.3 %copy-start.1 = (bf16[32,4608]{1,0:T(8,128)(2,1)S(1)}, bf16[32,4608]{1,0:T(8,128)(2,1)}, u32[]{:S(2)}) copy-start(bf16[32,4608]{1,0:T(8,128)(2,1)} %message.1.own) | copy-start | bytes 884740
  14.0 18.1 %collective-permute-start.1 = (bf16[64,4608]{1,0:T(8,128)(2,1)S(1)}, bf16[64,4608]{1,0:T(8,128)(2,1)S(1)}, u32[]{:S(2)}, u32[]{:S(2)}) collective-permute-start(bf16[64,4608]{1,0:T(8,128)(2,1)S(1)} %joined.1), channel_id=1, source_target_pairs={{2,0},{4,2},{6,4},{8,6},{10,8},{12,10},{14,12},{3,1},{5,3},{7,5},{... | collective-permute-start | bytes 1769480 | tf_op jit(solution)/shard_map/ppermute | solution.py:375
  42.0 25.6 %collective-permute-start.2 = (bf16[64,4096]{1,0:T(8,128)(2,1)S(1)}, bf16[64,4096]{1,0:T(8,128)(2,1)S(1)}, u32[]{:S(2)}, u32[]{:S(2)}) collective-permute-start(bf16[64,4096]{1,0:T(8,128)(2,1)S(1)} %get-tuple-element.28), channel_id=1, source_target_pairs={{0,4},{2,6},{4,8},{6,10},{8,12},{10,14},{1,5},{3,7},{5,9},{7,11},{... | collective-permute-start | bytes 1572872 | tf_op jit(solution)/shard_map/ppermute | solution.py:378
  67.7 8.1 %collective-permute-start.3 = (f32[32,4096]{1,0:T(8,128)S(1)}, f32[32,4096]{1,0:T(8,128)S(1)}, u32[]{:S(2)}, u32[]{:S(2)}) collective-permute-start(f32[32,4096]{1,0:T(8,128)S(1)} %get-tuple-element.32), channel_id=1, source_target_pairs={{0,1},{1,0},{2,3},{3,2},{4,5},{5,4},{6,7},{7,6},{8,9},{9,8},{10,11... | collective-permute-start | bytes 1572872 | tf_op jit(solution)/shard_map/ppermute | solution.py:441
  67.8 8.0 %collective-permute-start.4 = (bf16[32,4096]{1,0:T(8,128)(2,1)S(1)}, bf16[32,4096]{1,0:T(8,128)(2,1)S(1)}, u32[]{:S(2)}, u32[]{:S(2)}) collective-permute-start(bf16[32,4096]{1,0:T(8,128)(2,1)S(1)} %onward.1), channel_id=1, source_target_pairs={{0,2},{2,4},{4,6},{6,8},{8,10},{10,12},{12,14},{1,3},{3,5},{5,7},{... | collective-permute-start | bytes 786440 | tf_op jit(solution)/shard_map/ppermute | solution.py:378
